TPU v7x, 512 devices: a whole 4x4x16 slice. The times are simulated.
512 devices in a mesh: frames: 64 (over z, y_hi, core), mp: 4 (over x), dp: 2 (over y_lo).
Axes of the slice: x: 4, y: 4 (y_hi: 2, y_lo: 2; y = y_hi * 2 + y_lo), z: 16, core: 2. Of those that a mesh axis runs over, the one named last changes fastest.
Arguments:
- projections: bfloat16 [2, 128, 96, 3, 3584], P('dp', 'frames', None, None, 'mp'), may hold values from -18 to 18
- perturbation: bfloat16 [2, 128, 96, 3, 3584], P('dp', 'frames', None, None, 'mp'), may hold values from -44 to 44
- out_weight: bfloat16 [3584, 3584], P('frames', 'mp'), may hold values from -0.09375 to 0.09375
- norm_gain: float32 [3584], P('mp'), may hold values from 0.25 to 1.75
- live_counts: int32 [2, 128], P('dp'), may hold values from 72 to 96, as said below
Outputs:
- features: bfloat16 [2, 128, 96, 3584], P('dp', 'frames', None, 'mp')
- penalty: float32 [2], P('dp')
- gain_grad: float32 [3584], P('mp')
Inputs may be any that keep to these rules, and one draw needn't show every extreme that they name: `live_counts`: in each clip one slot has all 96 tokens live and another has 72 live.
All inputs are finite; a program needn't handle non-finite values.
Results may differ from a plain program's by a relative error of at most 0.0057.
Values may be sent and summed in bfloat16 or wider, within the bound.
A program may use at most 64 MiB of HBM per device.

v0:
```python
import math
import jax
import jax.numpy as jnp
from jax import lax
from jax.sharding import PartitionSpec as P

HEAD_DIM = 128
sigma_noise = 0.25
epsilon = 1e-06


def padded(cells, sides, width):
    for axis, dim in sides:
        count = lax.axis_size(axis)
        ends = count - 1
        head = lax.slice_in_dim(cells, 0, width, axis=dim)
        tail = lax.slice_in_dim(cells, cells.shape[dim] - width, cells.shape[dim], axis=dim)
        cells = jnp.concatenate(
            [
                lax.ppermute(tail, axis, [(i, (i + 1) % count) for i in range(ends)]),
                cells,
                lax.ppermute(head, axis, [((i + 1) % count, i) for i in range(ends)]),
            ],
            axis=dim,
        )
    return cells


def split_heads(tensor):
    return tensor.reshape(tensor.shape[:-1] + (tensor.shape[-1] // HEAD_DIM, HEAD_DIM))


def attend(query_rows, key_rows, value_rows, key_live):
    scores = jnp.einsum(
        "wrhe,wmhe->whrm",
        split_heads(query_rows),
        split_heads(key_rows),
        preferred_element_type=jnp.float32,
    ) * (1.0 / math.sqrt(HEAD_DIM))
    live_float = key_live[:, None, None, :]
    masked = jnp.where(live_float, scores, -1e30)
    largest = jnp.max(masked, axis=-1, keepdims=True)
    weights = jnp.exp(masked - largest) * live_float.astype(jnp.float32)
    probabilities = (weights / jnp.sum(weights, axis=-1, keepdims=True)).astype(jnp.bfloat16)
    mixed = jnp.einsum(
        "whrm,wmhe->wrhe",
        probabilities,
        split_heads(value_rows),
        preferred_element_type=jnp.float32,
    )
    return mixed.astype(jnp.bfloat16).reshape(query_rows.shape)


def attend_each(query_rows, key_rows, value_rows, key_live):

    def one_window(item):
        return attend(item[0][None], item[1][None], item[2][None], item[3][None])[0]

    return lax.map(one_window, (query_rows, key_rows, value_rows, key_live))


def local(projections, perturbation, out_weight, norm_gain, live_counts):
    tile_len = projections.shape[2]
    local_width = projections.shape[4]
    slab_count = lax.axis_size("frames")
    slab_index = lax.axis_index("frames")
    model_width = local_width * lax.axis_size("mp")
    token_total = projections.shape[1] * slab_count * tile_len
    perturbed = (
        projections.astype(jnp.float32) + sigma_noise * perturbation.astype(jnp.float32)
    ).astype(jnp.bfloat16)
    streams = jnp.concatenate([projections, perturbed], axis=0)
    padded_counts = jnp.pad(live_counts[0], (1, 1))
    nearby = lax.dynamic_slice_in_dim(padded_counts, 2 * slab_index, 4)
    token_pos = jnp.arange(tile_len)
    live_near = token_pos[None, :] < nearby[:, None]
    key_values = streams[:, :, :, 1:, :]
    widened = padded(key_values, (("frames", 1),), 1)
    grouped = widened.reshape(4, 2 * tile_len, 2, local_width)
    query_rows = streams[:, :, :, 0, :].reshape(4, tile_len, local_width)
    key_live = jnp.tile(live_near.reshape(2, 2 * tile_len), (2, 1))
    attended = attend_each(query_rows, grouped[:, :, 0], grouped[:, :, 1], key_live)
    attended = attended.reshape(2, 2, tile_len, local_width)
    gathered = lax.all_gather(attended, "mp", axis=3, tiled=True)
    flat_rows = gathered.reshape(-1, model_width)
    projected = jnp.dot(
        flat_rows,
        lax.all_gather(out_weight, "frames", axis=0, tiled=True),
        preferred_element_type=jnp.float32,
    )
    projected = projected.reshape(2, 2, tile_len, local_width)
    squares = lax.psum(jnp.sum(projected * projected, axis=-1), "mp")
    normed = projected * lax.rsqrt(squares / model_width + epsilon)[..., None]
    own_live = live_near[1:3].astype(jnp.float32)[:, :, None]
    features = (normed[0] * norm_gain * own_live).astype(jnp.bfloat16)[None]
    difference = (normed[1] - normed[0]) * own_live
    feature_sums = jnp.sum(difference * difference, axis=(0, 1))
    local_penalty = jnp.sum(feature_sums * norm_gain * norm_gain).reshape(1)
    penalty = lax.psum(local_penalty, ("frames", "mp")) / (
        sigma_noise * sigma_noise * token_total * model_width
    )
    gain_grad = (
        norm_gain
        * lax.psum(feature_sums, ("frames", "dp"))
        / (sigma_noise * sigma_noise * token_total)
    )
    return (features, penalty, gain_grad)


def solution(mesh):
    placed = (
        P("dp", "frames", None, None, "mp"),
        P("dp", "frames", None, None, "mp"),
        P("frames", "mp"),
        P("mp"),
        P("dp", None),
    )
    return jax.shard_map(
        local,
        mesh=mesh,
        in_specs=placed,
        out_specs=(P("dp", "frames", None, "mp"), P("dp"), P("mp")),
        check_vma=False,
    )
```

profile of v0, /device:TPU:2, one launch (start us, length us, event | category | flops | bytes accessed | tf_op | source)
XLA Modules:
  0.0 1192.0 jit_solution(10483000948008665854)
XLA Ops:
  7.2 1.9 add_convert_fusion
  9.2 1.2 fusion.25
  10.4 2.6 collective-permute-start
  13.0 1.3 collective-permute-start.1
  15.0 4.5 collective-permute-done.1
  19.5 1.7 pad_maximum_fusion
  21.2 0.3 copy.13
  21.5 1.3 slice_bitcast_fusion
  22.8 22.9 %while.10 = (s32[]{:T(128)}, bf16[4,96,896]{2,1,0:T(8,128)(2,1)}, bf16[4,192,896]{2,1,0:T(8,128)(2,1)}, pred[4,192]{1,0:T(4,128)(4,1)S(1)}, bf16[4,96,896]{2,1,0...) while((s32[]{:T(128)}, bf16[4,96,896]{2,1,0:T(8,128)(2,1)}, bf16[4,192,896]{2,1,0:T(8,128)(2,1)}, ...), condition=%wide.region_3.4_spmd, body=%wide.region_0.3_spmd.sunk | while | flops 67049856 | bytes 5857369 | solution.py:59
  22.8 1.0 constant_dynamic-slice_fusion.5
  23.8 0.4 reshape.106
  24.3 0.2 reshape.107
  24.5 1.5 fusion.45
  26.0 0.4 reshape.108
  26.4 1.4 fusion.46
  27.8 0.7 bitcast_dynamic-update-slice_fusion.2
  28.5 1.0 constant_dynamic-slice_fusion.5
  29.5 0.4 reshape.106
  30.0 0.2 reshape.107
  30.2 1.5 fusion.45
  31.7 0.4 reshape.108
  32.1 1.4 fusion.46
  33.5 0.7 bitcast_dynamic-update-slice_fusion.2
  34.2 1.0 constant_dynamic-slice_fusion.5
  35.3 0.4 reshape.106
  35.7 0.2 reshape.107
  36.0 1.5 fusion.45
  37.5 0.4 reshape.108
  37.9 1.4 fusion.46
  39.3 0.7 bitcast_dynamic-update-slice_fusion.2
  40.0 1.0 constant_dynamic-slice_fusion.5
  41.0 0.4 reshape.106
  41.5 0.2 reshape.107
  41.7 1.5 fusion.45
  43.2 0.4 reshape.108
  43.6 1.4 fusion.46
  45.0 0.7 bitcast_dynamic-update-slice_fusion.2
  45.8 0.7 all-gather.5.cloned.1.call-update
  46.5 59.2 %all-gather.3.cloned.1.call-done = bf16[2,2,96,3584]{3,2,1,0:T(8,128)(2,1)} async-done(((bf16[2,2,96,896]{3,2,1,0:T(8,128)(2,1)}), bf16[2,2,96,3584]{3,2,1,0:T(8,128)(2,1)}) %all-gather.3.cloned.1.call-update) | async-done | bytes 2752528 | tf_op jit(solution)/shard_map/all_gather | solution.py:84
  105.8 162.8 %all-gather.5.cloned.1.call-done = bf16[3584,896]{1,0:T(8,128)(2,1)} async-done(((bf16[56,896]{1,0:T(8,128)(2,1)}), bf16[3584,896]{1,0:T(8,128)(2,1)}) %all-gather.5.cloned.1.call-update) | async-done | bytes 6422544 | tf_op jit(solution)/shard_map/all_gather | solution.py:88
  268.6 6.7 multiply_reduce_fusion
  275.3 8.6 psum.21
  283.9 0.2 broadcast_multiply_fusion
  284.1 0.2 fusion.29
  284.3 247.6 %psum.23 = f32[896]{0:T(1024)S(1)} all-reduce(f32[896]{0:T(1024)S(1)} %fusion.29), channel_id=1, replica_groups=mesh['frames'=64,'mp'=4,'dp'=2] {'frames','dp'}, use_global_device_ids=true, to_apply=%region_9.10 | all-reduce | flops 896 | bytes 7168 | tf_op jit(solution)/shard_map/psum | solution.py:104
  532.0 0.8 multiply_convert_fusion
  532.8 1.2 multiply_multiply_fusion.1
  534.0 649.4 %psum.22 = f32[1]{0:T(128)} all-reduce(f32[1]{0:T(128)} %bitcast.11), channel_id=1, replica_groups=mesh['frames'=64,'mp'=4,'dp'=2] {'frames','mp'}, use_global_device_ids=true, to_apply=%region_8.9 | all-reduce | flops 1 | bytes 8 | tf_op jit(solution)/shard_map/psum | solution.py:99
  (37 shorter events, 1.1 us)
Async XLA Ops:
  7.2 2.0 copy-start
  7.2 98.6 %all-gather.3.cloned.1.call-start = ((), (), s32[]{:S(2)}) async-start(), calls=%async_computation | async-start | bytes 3440640 | tf_op jit(solution)/shard_map/all_gather | solution.py:84
  9.2 5.1 copy-start.2
  10.4 4.6 collective-permute-start
  13.0 6.5 collective-permute-start.1
  45.7 222.9 %all-gather.5.cloned.1.call-start = ((), (), s32[]{:S(2)}) async-start(), calls=%async_computation.1 | async-start | bytes 6522880 | tf_op jit(solution)/shard_map/all_gather | solution.py:88
  283.9 248.0 %copy-start.1 = (f32[896]{0:T(1024)S(1)}, f32[896]{0:T(1024)}, u32[]{:S(2)}) copy-start(f32[896]{0:T(1024)} %param.10) | copy-start | bytes 10756
Sparse Core Ops, SparseCore 0:
  45.8 59.8 all-gather.2
  109.0 159.5 all-gather.4
where the time goes:
time: 1190 us
  blocking collectives  906 us (76%)
  waiting for transfers between devices  227 us (19%)
  matrix products  18.3 us (2%)
  between operations  15.9 us (1%)
  local copies, waits for them, and re-layouts  13.2 us (1%)
    psum x1, blocking collectives, local(): lax.psum(local_penalty, ('frames', 'mp'))  649 us
    psum x1, blocking collectives, local(): lax.psum(feature_sums, ('frames', 'dp'))  248 us
    all_gather x1, waiting for transfers between devices, local(): lax.all_gather(out_weight, 'frames', axis=0, tiled=True)  163 us
    all_gather x1, waiting for transfers between devices, local(): gathered = lax.all_gather(attended, 'mp', axis=3, tiled=True)  59.2 us
  transfers between devices with their start and end apart: 4, of which 3 were waited for; matrix products, arithmetic and copies ran while one was open for 0% of the time, Pallas kernels for 0%

commit v1 on v0

--- a/solution.py
+++ b/solution.py
@@ -96,7 +96,7 @@
     difference = (normed[1] - normed[0]) * own_live
     feature_sums = jnp.sum(difference * difference, axis=(0, 1))
     local_penalty = jnp.sum(feature_sums * norm_gain * norm_gain).reshape(1)
-    penalty = lax.psum(local_penalty, ("frames", "mp")) / (
+    penalty = lax.psum(lax.psum(local_penalty, "mp"), "frames") / (
         sigma_noise * sigma_noise * token_total * model_width
     )
     gain_grad = (

time: 1190 us -> 684 us (0.57)
  the two profiles are of different devices: /device:TPU:2 before, /device:TPU:1 now
where the time goes in v1:
time: 684 us; the launch traced here: 683 us
  blocking collectives  395 us (58%)
  waiting for transfers between devices  221 us (32%)
  matrix products  18.3 us (3%)
  between operations  15.9 us (2%)
  local copies, waits for them, and re-layouts  13.2 us (2%)
  starting transfers between devices  11 us (2%)
  other arithmetic  7.59 us (1%)
    psum x1, blocking collectives, local(): lax.psum(feature_sums, ('frames', 'dp'))  247 us
    all_gather x1, waiting for transfers between devices, local(): lax.all_gather(out_weight, 'frames', axis=0, tiled=True)  162 us
    psum x1, blocking collectives, local(): lax.psum(lax.psum(local_penalty, 'mp'), 'frames')  133 us
    all_gather x1, waiting for transfers between devices, local(): gathered = lax.all_gather(attended, 'mp', axis=3, tiled=True)  48.2 us
  transfers between devices with their start and end apart: 4, of which 3 were waited for; matrix products, arithmetic and copies ran while one was open for 0% of the time, Pallas kernels for 0%

profile of v1, /device:TPU:1, one launch (start us, length us, event | category | flops | bytes accessed | tf_op | source)
XLA Modules:
  0.0 683.1 jit_solution(6552076949508623243)
XLA Ops:
  7.2 1.9 add_convert_fusion
  9.2 1.2 fusion.25
  10.4 6.2 collective-permute-start
  16.6 4.7 collective-permute-start.1
  22.0 10.1 %collective-permute-done = bf16[2,1,96,2,896]{4,2,3,1,0:T(8,128)(2,1)} collective-permute-done((bf16[2,1,96,2,896]{4,2,3,1,0:T(8,128)(2,1)}, bf16[2,1,96,2,896]{4,2,3,1,0:T(8,128)(2,1)}, u32[]{:S(2)}, u32[]{:S(2)}) %collective-permute-start) | collective-permute-done | bytes 688160 | tf_op jit(solution)/shard_map/ppermute | solution.py:20
  32.2 1.7 pad_maximum_fusion
  33.8 0.3 copy.13
  34.1 1.3 slice_bitcast_fusion
  35.4 22.9 %while.10 = (s32[]{:T(128)}, bf16[4,96,896]{2,1,0:T(8,128)(2,1)}, bf16[4,192,896]{2,1,0:T(8,128)(2,1)}, pred[4,192]{1,0:T(4,128)(4,1)S(1)}, bf16[4,96,896]{2,1,0...) while((s32[]{:T(128)}, bf16[4,96,896]{2,1,0:T(8,128)(2,1)}, bf16[4,192,896]{2,1,0:T(8,128)(2,1)}, ...), condition=%wide.region_3.4_spmd, body=%wide.region_0.3_spmd.sunk | while | flops 67049856 | bytes 5857369 | solution.py:59
  35.4 1.0 constant_dynamic-slice_fusion.5
  36.5 0.4 reshape.106
  37.0 0.2 reshape.107
  37.2 1.5 fusion.45
  38.7 0.4 reshape.108
  39.1 1.4 fusion.46
  40.5 0.7 bitcast_dynamic-update-slice_fusion.2
  41.2 1.0 constant_dynamic-slice_fusion.5
  42.2 0.4 reshape.106
  42.7 0.2 reshape.107
  42.9 1.5 fusion.45
  44.4 0.4 reshape.108
  44.8 1.4 fusion.46
  46.2 0.7 bitcast_dynamic-update-slice_fusion.2
  46.9 1.0 constant_dynamic-slice_fusion.5
  47.9 0.4 reshape.106
  48.4 0.2 reshape.107
  48.6 1.5 fusion.45
  50.1 0.4 reshape.108
  50.5 1.4 fusion.46
  51.9 0.7 bitcast_dynamic-update-slice_fusion.2
  52.6 1.0 constant_dynamic-slice_fusion.5
  53.7 0.4 reshape.106
  54.1 0.2 reshape.107
  54.4 1.5 fusion.45
  55.9 0.4 reshape.108
  56.3 1.4 fusion.46
  57.7 0.7 bitcast_dynamic-update-slice_fusion.2
  58.4 0.7 all-gather.5.cloned.1.call-update
  59.2 48.2 %all-gather.3.cloned.1.call-done = bf16[2,2,96,3584]{3,2,1,0:T(8,128)(2,1)} async-done(((bf16[2,2,96,896]{3,2,1,0:T(8,128)(2,1)}), bf16[2,2,96,3584]{3,2,1,0:T(8,128)(2,1)}) %all-gather.3.cloned.1.call-update) | async-done | bytes 2752528 | tf_op jit(solution)/shard_map/all_gather | solution.py:84
  107.5 162.4 %all-gather.5.cloned.1.call-done = bf16[3584,896]{1,0:T(8,128)(2,1)} async-done(((bf16[56,896]{1,0:T(8,128)(2,1)}), bf16[3584,896]{1,0:T(8,128)(2,1)}) %all-gather.5.cloned.1.call-update) | async-done | bytes 6422544 | tf_op jit(solution)/shard_map/all_gather | solution.py:88
  269.9 6.7 multiply_reduce_fusion
  276.6 8.4 %psum.28 = f32[2,2,96]{2,1,0:T(2,128)S(1)} all-reduce(f32[2,2,96]{2,1,0:T(2,128)S(1)} %get-tuple-element.58), channel_id=1, replica_groups=mesh['frames'=64,'mp'=4,'dp'=2] {'mp'}, use_global_device_ids=true, to_apply=%region_5.6 | all-reduce | flops 384 | bytes 3072 | tf_op jit(solution)/shard_map/psum | solution.py:92
  285.2 0.2 fusion.29
  285.4 247.0 %psum.31 = f32[896]{0:T(1024)S(1)} all-reduce(f32[896]{0:T(1024)S(1)} %fusion.29), channel_id=1, replica_groups=mesh['frames'=64,'mp'=4,'dp'=2] {'frames','dp'}, use_global_device_ids=true, to_apply=%region_10.11 | all-reduce | flops 896 | bytes 7168 | tf_op jit(solution)/shard_map/psum | solution.py:104
  532.5 1.2 multiply_multiply_fusion.1
  533.7 6.6 psum.29
  540.3 0.8 multiply_convert_fusion
  541.1 133.3 %psum.30 = f32[1]{0:T(128)} all-reduce(f32[1]{0:T(128)} %psum.29), channel_id=1, replica_groups=mesh['frames'=64,'mp'=4,'dp'=2] {'frames'}, use_global_device_ids=true, to_apply=%region_9.10 | all-reduce | flops 1 | bytes 8 | tf_op jit(solution)/shard_map/psum | solution.py:99
  (38 shorter events, 1.3 us)
Async XLA Ops:
  7.2 2.0 copy-start
  7.2 100.3 %all-gather.3.cloned.1.call-start = ((), (), s32[]{:S(2)}) async-start(), calls=%async_computation | async-start | bytes 3440640 | tf_op jit(solution)/shard_map/all_gather | solution.py:84
  9.2 12.2 %copy-start.2 = (s32[1,128]{1,0:T(1,128)S(1)}, s32[1,128]{1,0:T(1,128)}, u32[]{:S(2)}) copy-start(s32[1,128]{1,0:T(1,128)} %param.11) | copy-start | bytes 1540
  10.4 21.8 %collective-permute-start = (bf16[2,1,96,2,896]{4,2,3,1,0:T(8,128)(2,1)}, bf16[2,1,96,2,896]{4,2,3,1,0:T(8,128)(2,1)}, u32[]{:S(2)}, u32[]{:S(2)}) collective-permute-start(bf16[2,1,96,2,896]{4,2,3,1,0:T(8,128)(2,1)} %get-tuple-element.54), channel_id=1, source_target_pairs={{0,8},{8,16},{16,24},{24,32},{32,40},{40,48},{48,56},{56,64},{64,7... | collective-permute-start | bytes 2064392 | tf_op jit(solution)/shard_map/ppermute | solution.py:20
  16.6 15.6 %collective-permute-start.1 = (bf16[2,1,96,2,896]{4,2,3,1,0:T(8,128)(2,1)}, bf16[2,1,96,2,896]{4,2,3,1,0:T(8,128)(2,1)}, u32[]{:S(2)}, u32[]{:S(2)}) collective-permute-start(bf16[2,1,96,2,896]{4,2,3,1,0:T(8,128)(2,1)} %get-tuple-element.55), channel_id=1, source_target_pairs={{8,0},{16,8},{24,16},{32,24},{40,32},{48,40},{56,48},{64,56},{72,6... | collective-permute-start | bytes 2064392 | tf_op jit(solution)/shard_map/ppermute | solution.py:22
  58.4 211.5 %all-gather.5.cloned.1.call-start = ((), (), s32[]{:S(2)}) async-start(), calls=%async_computation.1 | async-start | bytes 6522880 | tf_op jit(solution)/shard_map/all_gather | solution.py:88
  285.0 247.4 %copy-start.1 = (f32[896]{0:T(1024)S(1)}, f32[896]{0:T(1024)}, u32[]{:S(2)}) copy-start(f32[896]{0:T(1024)} %param.10) | copy-start | bytes 10756
Sparse Core Ops, SparseCore 0:
  58.5 48.9 all-gather.2
  110.6 159.1 all-gather.4

commit v2 on v0

--- a/solution.py
+++ b/solution.py
@@ -85,7 +85,10 @@
     flat_rows = gathered.reshape(-1, model_width)
     projected = jnp.dot(
         flat_rows,
-        lax.all_gather(out_weight, "frames", axis=0, tiled=True),
+        jnp.concatenate(
+            lax.all_to_all(jnp.stack([out_weight] * lax.axis_size("frames")), "frames", 0, 0),
+            axis=0,
+        ),
         preferred_element_type=jnp.float32,
     )
     projected = projected.reshape(2, 2, tile_len, local_width)

time: 1190 us -> 1310 us (1.10)
  waiting for transfers between devices: 227 us -> 322 us
  starting transfers between devices: 3.95 us -> 23.1 us
    all_gather x1, waiting for transfers between devices: 59.2 us -> 317 us  [local(): gathered = lax.all_gather(attended, 'mp', axis=3, tiled=True)]
    all_gather x1 -> x0, waiting for transfers between devices: 163 us -> none  [local(): lax.all_gather(out_weight, 'frames', axis=0, tiled=True)]
    all_to_all x0 -> x1, starting transfers between devices: none -> 19.1 us  [local(): lax.all_to_all(jnp.stack([out_weight] * lax.axis_size('frames')), 'frames...]
  transfers between devices with their start and end apart: 4 -> 4, of which waited for: 3 -> 2; matrix products, arithmetic and copies ran while one was open for 0% -> 2% of each run, Pallas kernels for 0% -> 0%
where the time goes in v2:
time: 1310 us
  blocking collectives  908 us (69%)
  waiting for transfers between devices  322 us (25%)
  starting transfers between devices  23.1 us (2%)
  matrix products  18.1 us (1%)
  local copies, waits for them, and re-layouts  17.4 us (1%)
  between operations  15.9 us (1%)
    psum x1, blocking collectives, local(): lax.psum(local_penalty, ('frames', 'mp'))  648 us
    all_gather x1, waiting for transfers between devices, local(): gathered = lax.all_gather(attended, 'mp', axis=3, tiled=True)  317 us
    psum x1, blocking collectives, local(): lax.psum(feature_sums, ('frames', 'dp'))  250 us
  transfers between devices with their start and end apart: 4, of which 2 were waited for; matrix products, arithmetic and copies ran while one was open for 2% of the time, Pallas kernels for 0%

profile of v2, /device:TPU:2, one launch (start us, length us, event | category | flops | bytes accessed | tf_op | source)
XLA Modules:
  0.0 1309.9 jit_solution(1644639028979235806)
XLA Ops:
  7.2 4.1 stack.2
  11.2 19.1 %all-to-all-start = ((bf16[64,56,896]{2,1,0:T(8,128)(2,1)}), bf16[64,56,896]{2,1,0:T(8,128)(2,1)}, u32[]{:S(2)}, u32[]{:S(2)}) async-start(bf16[64,56,896]{2,1,0:T(8,128)(2,1)} %stack.2), calls=%async_computation | async-start | bytes 12845056 | tf_op jit(solution)/shard_map/all_to_all | solution.py:89
  30.4 0.3 add_convert_fusion
  30.7 1.3 fusion.23
  32.0 2.7 collective-permute-start
  34.7 1.3 collective-permute-start.1
  36.8 4.2 collective-permute-done.1
  40.9 1.7 pad_maximum_fusion
  42.6 0.3 copy.13
  42.9 1.4 slice_bitcast_fusion
  44.3 22.7 %while.10 = (s32[]{:T(128)}, bf16[4,96,896]{2,1,0:T(8,128)(2,1)}, bf16[4,192,896]{2,1,0:T(8,128)(2,1)}, pred[4,192]{1,0:T(4,128)(4,1)S(1)}, bf16[4,96,896]{2,1,0...) while((s32[]{:T(128)}, bf16[4,96,896]{2,1,0:T(8,128)(2,1)}, bf16[4,192,896]{2,1,0:T(8,128)(2,1)}, ...), condition=%wide.region_3.4_spmd, body=%wide.region_0.3_spmd.sunk | while | flops 67049856 | bytes 5857369 | solution.py:59
  44.3 1.0 constant_dynamic-slice_fusion.5
  45.3 0.4 reshape.112
  45.8 0.2 reshape.113
  46.0 1.4 fusion.44
  47.5 0.4 reshape.114
  47.9 1.4 fusion.45
  49.3 0.7 bitcast_dynamic-update-slice_fusion.2
  50.0 1.0 constant_dynamic-slice_fusion.5
  51.0 0.4 reshape.112
  51.5 0.2 reshape.113
  51.7 1.4 fusion.44
  53.2 0.4 reshape.114
  53.6 1.4 fusion.45
  55.0 0.7 bitcast_dynamic-update-slice_fusion.2
  55.7 1.0 constant_dynamic-slice_fusion.5
  56.7 0.4 reshape.112
  57.2 0.2 reshape.113
  57.4 1.4 fusion.44
  58.8 0.4 reshape.114
  59.2 1.4 fusion.45
  60.7 0.7 bitcast_dynamic-update-slice_fusion.2
  61.3 1.0 constant_dynamic-slice_fusion.5
  62.4 0.4 reshape.112
  62.9 0.2 reshape.113
  63.1 1.4 fusion.44
  64.5 0.4 reshape.114
  64.9 1.4 fusion.45
  66.3 0.7 bitcast_dynamic-update-slice_fusion.2
  67.1 317.4 %all-gather.2.cloned.1.call-done = bf16[2,2,96,3584]{3,2,1,0:T(8,128)(2,1)} async-done(((bf16[2,2,96,896]{3,2,1,0:T(8,128)(2,1)}), bf16[2,2,96,3584]{3,2,1,0:T(8,128)(2,1)}) %all-gather.2.cloned.1.call-update) | async-done | bytes 2752528 | tf_op jit(solution)/shard_map/all_gather | solution.py:84
  384.5 6.7 multiply_reduce_fusion
  391.3 9.1 psum.21
  400.4 0.2 broadcast_multiply_fusion
  400.6 0.2 fusion.27
  400.8 250.4 %psum.23 = f32[896]{0:T(1024)S(1)} all-reduce(f32[896]{0:T(1024)S(1)} %fusion.27), channel_id=1, replica_groups=mesh['frames'=64,'mp'=4,'dp'=2] {'frames','dp'}, use_global_device_ids=true, to_apply=%region_9.10 | all-reduce | flops 896 | bytes 7168 | tf_op jit(solution)/shard_map/psum | solution.py:107
  651.3 0.8 multiply_convert_fusion
  652.1 1.2 multiply_multiply_fusion.1
  653.3 648.0 %psum.22 = f32[1]{0:T(128)} all-reduce(f32[1]{0:T(128)} %bitcast.12), channel_id=1, replica_groups=mesh['frames'=64,'mp'=4,'dp'=2] {'frames','mp'}, use_global_device_ids=true, to_apply=%region_8.9 | all-reduce | flops 1 | bytes 8 | tf_op jit(solution)/shard_map/psum | solution.py:102
  (39 shorter events, 1.1 us)
Async XLA Ops:
  11.2 19.2 %copy-start = (bf16[1,2,96,3,896]{4,2,3,1,0:T(8,128)(2,1)S(1)}, bf16[1,2,96,3,896]{4,2,3,1,0:T(8,128)(2,1)}, u32[]{:S(2)}) copy-start(bf16[1,2,96,3,896]{4,2,3,1,0:T(8,128)(2,1)} %param.7) | copy-start | bytes 3096580
  11.2 19.2 %copy-start.1 = (bf16[1,2,96,3,896]{4,2,3,1,0:T(8,128)(2,1)S(1)}, bf16[1,2,96,3,896]{4,2,3,1,0:T(8,128)(2,1)}, u32[]{:S(2)}) copy-start(bf16[1,2,96,3,896]{4,2,3,1,0:T(8,128)(2,1)} %param.8) | copy-start | bytes 3096580
  11.2 373.3 %all-to-all-start = ((bf16[64,56,896]{2,1,0:T(8,128)(2,1)}), bf16[64,56,896]{2,1,0:T(8,128)(2,1)}, u32[]{:S(2)}, u32[]{:S(2)}) async-start(bf16[64,56,896]{2,1,0:T(8,128)(2,1)} %stack.2), calls=%async_computation | async-start | bytes 12845056 | tf_op jit(solution)/shard_map/all_to_all | solution.py:89
  30.3 354.2 %all-gather.2.cloned.1.call-start = ((), (), s32[]{:S(2)}) async-start(), calls=%async_computation.1 | async-start | bytes 3440640 | tf_op jit(solution)/shard_map/all_gather | solution.py:84
  30.7 5.3 copy-start.3
  32.0 4.7 collective-permute-start
  34.7 6.2 collective-permute-start.1
  400.4 250.9 %copy-start.2 = (f32[896]{0:T(1024)S(1)}, f32[896]{0:T(1024)}, u32[]{:S(2)}) copy-start(f32[896]{0:T(1024)} %param.10) | copy-start | bytes 10756
Sparse Core Ops, SparseCore 0:
  67.2 317.3 all-gather.1
